TPU v7x, 256 devices: a whole 4x4x8 slice. The times are simulated.
256 devices in a mesh: dom: 16 (over z, core), hour: 16 (over y, x).
Axes of the slice: x: 4, y: 4, z: 8, core: 2. Of those that a mesh axis runs over, the one named last changes fastest.
Arguments:
- inc_local: float32 [16384, 2048], P('dom'), may hold values from -0.125 to 0.125
- inc_bound: float32 [8192, 2048], P('dom'), may hold values from -0.125 to 0.125
- bound_rows: int32 [16, 16, 32], P('dom'), may hold values from 0 to 1023
- bound_count: int32 [16, 16], replicated, may hold values from 0 to 32, as said below
- block_presence_mask: int32 [64, 8], P('dom'), may hold values 0 or 1
- stor_nodes: int32 [16, 128], P('dom'), may hold values from 0 to 1023
- flow0: float32 [32768, 2048], P('dom', 'hour'), may hold values from 0 to 1
- stor0: float32 [2048, 2048], P('dom', 'hour'), may hold values from 0 to 2
- dual0: float32 [16384, 2048], P('dom', 'hour'), may hold values from -6 to 6
- demand: float32 [16384, 2048], P('dom', 'hour'), may hold values from -6 to 6
- pipe_cost: float32 [32768], P('dom'), may hold values from 0.3 to 3
- pipe_cap: float32 [32768], P('dom'), may hold values from 0.5 to 2
- stor_cost: float32 [2048], P('dom'), may hold values from 0.3 to 3
- stor_cap: float32 [2048], P('dom'), may hold values from 1 to 4
Outputs:
- flow: float32 [32768, 2048], P('dom', 'hour')
- level: float32 [2048, 2048], P('dom', 'hour')
- dual: float32 [16384, 2048], P('dom', 'hour')
Inputs may be any that keep to these rules, and one draw needn't show every extreme that they name: bound_count[o][q] is 0 where o = q; every owner o has one peer with exactly 32 live slots.
All inputs are finite; a program needn't handle non-finite values. No bound on the sum of `block_presence_mask` on one device may be relied on, other than what follows from the above.
Results may differ from a plain program's by a relative error of at most 0.0001.
Values sent between devices are 32-bit elements; how exact they have to be, the bound alone decides.
A program may use at most 128 MiB of HBM per device.

v0:
```python
import jax
import jax.numpy as jnp
from jax import lax
from jax.experimental import pallas as pl
from jax.experimental.pallas import tpu as pltpu
from jax.sharding import PartitionSpec as P

ITERS = 2
STEP = 0.3
HALVES = 2
MESH = pl.DeviceIdType.MESH
F32 = jnp.float32
BF16 = jnp.bfloat16
NN = (((1,), (0,)), ((), ()))
NT = (((1,), (1,)), ((), ()))

GROUPS = (
    ((4, 0), (4, 1), (3, 0), (3, 1), (-3, 0), (-3, 1), (0, 1), (0, 0)),
    ((2, 0), (2, 1), (-2, 0), (-2, 1), (1, 0), (1, 1), (-1, 0), (-1, 1)),
)
BLOCKS = GROUPS[0] + GROUPS[1]
PER = len(GROUPS[0])
OWN = BLOCKS.index((0, 0))
MIRROR = [BLOCKS.index((4 if dz == 4 else -dz, flip)) for dz, flip in BLOCKS]


def dot(a, b, dims):
    return lax.dot_general(a, b, dims, preferred_element_type=F32)


def parts(x):
    hi = x.astype(BF16)
    lo = (x - hi.astype(F32)).astype(BF16)
    return hi, lo


def product(hi, lo, mat_hi, mat_lo, dims):
    n = hi.shape[0]
    both = dot(jnp.concatenate([hi, lo], axis=0), mat_hi, dims)
    return both[:n] + both[n:] + dot(hi, mat_lo, dims)


def exact(hi, lo, onehot, dims):
    n = hi.shape[0]
    both = dot(jnp.concatenate([hi, lo], axis=0), onehot, dims)
    return both[:n] + both[n:]


def swap_blocks(blocks, slots):
    count = len(blocks)
    group = lax.broadcasted_iota(jnp.int32, blocks[0].shape, 1) // slots
    result = []
    for i in range(count):
        out = blocks[i]
        for j in range(count):
            if j != i:
                out = jnp.where(group == j, pltpu.roll(blocks[j], ((j - i) % count) * slots, 1), out)
        result.append(out)
    return result


def kernel(
    inc_local, inc_bound, bound_rows, bound_count, presence, stor_nodes,
    flow0, stor0, dual0, demand, pipe_cost, pipe_cap, stor_cost, stor_cap,
    flow_out, level_out, dual_out,
    loc32, bnd32, loc_hi, loc_lo, bnd_hi, bnd_lo,
    nat_f, nat_y, nat_d, nat_s, rows_v, stor_v, cost_v, cap_v, scost_v, scap_v, count_s, pres_s,
    f_t, y_t, d_t, s_t, g_t, fb, yb, sd, onehot, live, w_t,
    send, recv, halo_send, halo_recv,
    in_sem, loc_sem, bnd_sem, out_sem, send_sem, recv_sem, halo_send_sem, halo_recv_sem,
):
    me = lax.axis_index("dom")
    hour = lax.axis_index("hour")
    hours = lax.axis_size("hour")
    nodes, pipes = inc_local.shape
    slots = bound_rows.shape[1]
    store = stor_nodes.shape[1]
    width = flow0.shape[1]
    half = width // HALVES
    msg = half * slots // 128
    per_tile = 128 // slots
    cols = PER * slots
    all_slots = 2 * cols

    def dom_at(dz, flip):
        z, core = me // 2, lax.rem(me, 2)
        z = lax.rem(z + (dz + 8), 8)
        return z * 2 + (1 - core if flip else core)

    nxt = lax.rem(hour + 1, hours)
    prv = lax.rem(hour + hours - 1, hours)

    barrier = pltpu.get_barrier_semaphore()
    for j, (dz, flip) in enumerate(BLOCKS):
        if j != OWN:
            pl.semaphore_signal(barrier, inc=1, device_id={"dom": dom_at(dz, flip)}, device_id_type=MESH)
    pl.semaphore_signal(barrier, inc=1, device_id={"hour": nxt}, device_id_type=MESH)
    pl.semaphore_signal(barrier, inc=1, device_id={"hour": prv}, device_id_type=MESH)

    ins = [
        (dual0, nat_y), (bound_rows, rows_v), (stor_nodes, stor_v), (bound_count, count_s), (presence, pres_s),
        (pipe_cost, cost_v), (pipe_cap, cap_v), (stor_cost, scost_v), (stor_cap, scap_v), (stor0, nat_s),
        (flow0, nat_f), (demand, nat_d),
    ]
    in_copies = [pltpu.make_async_copy(a, b, in_sem.at[i]) for i, (a, b) in enumerate(ins)]
    (cp_y, cp_rows, cp_stor, cp_count, cp_pres, cp_cost, cp_cap, cp_scost, cp_scap, cp_s, cp_f, cp_d) = in_copies
    n_loc = loc_sem.shape[0]
    n_bnd = bnd_sem.shape[0]
    step_loc = nodes // n_loc
    step_bnd = inc_bound.shape[0] // n_bnd

    def loc_copy(i):
        s = pl.ds(pl.multiple_of(i * step_loc, step_loc), step_loc)
        return pltpu.make_async_copy(inc_local.at[s], loc32.at[s], loc_sem.at[i])

    def bnd_copy(i):
        s = pl.ds(pl.multiple_of(i * step_bnd, step_bnd), step_bnd)
        return pltpu.make_async_copy(inc_bound.at[s], bnd32.at[s], bnd_sem.at[i])

    for c in in_copies[:10]:
        c.start()
    for i in range(n_loc):
        loc_copy(i).start()
    cp_f.start()
    for i in range(n_bnd):
        bnd_copy(i).start()
    cp_d.start()

    zero = jnp.zeros((msg, 128), F32)
    for x in range(2 * ITERS):
        for h in range(HALVES):
            recv[x, h, OWN * msg : (OWN + 1) * msg, :] = zero

    cp_rows.wait()
    cp_stor.wait()
    node = lax.broadcasted_iota(jnp.int32, (nodes, 128), 0)
    for t in range(all_slots // 128):
        pieces = [rows_v[pl.ds(dom_at(*BLOCKS[t * per_tile + p]), 1), :] for p in range(per_tile)]
        row = jnp.concatenate(pieces, axis=1)
        onehot[:, t * 128 : (t + 1) * 128] = jnp.where(node == row, 1.0, 0.0).astype(BF16)
    onehot[:, all_slots:] = jnp.where(node == stor_v[...], 1.0, 0.0).astype(BF16)

    cp_count.wait()
    lane = lax.broadcasted_iota(jnp.int32, (8, 128), 1)
    for t in range(all_slots // 128):
        counts = jnp.zeros((8, 128), jnp.int32)
        for p in range(per_tile):
            counts = jnp.where(lane // slots == p, count_s[dom_at(*BLOCKS[t * per_tile + p]), me], counts)
        live[:, t * 128 : (t + 1) * 128] = jnp.where(lax.rem(lane, slots) < counts, 1.0, 0.0).astype(F32)

    cp_y.wait()
    for j in range(nodes // 128):
        s = slice(j * 128, (j + 1) * 128)
        y_t[:, s] = nat_y[s, :].T
    hi, lo = parts(y_t[...])
    yb[:width, :] = hi
    yb[width:, :] = lo

    def rows_of(h):
        return pl.ds(pl.multiple_of(h * half, half), half)

    def lows_of(h):
        return pl.ds(pl.multiple_of(width + h * half, half), half)

    def message(x, h, j):
        dz, flip = BLOCKS[j]
        k = MIRROR[j]
        return pltpu.make_async_remote_copy(
            src_ref=send.at[x, h, pl.ds(j * msg, msg)],
            dst_ref=recv.at[x, h, pl.ds(k * msg, msg)],
            send_sem=send_sem.at[x, h, j // PER],
            recv_sem=recv_sem.at[x, h, k // PER],
            device_id={"dom": dom_at(dz, flip)},
            device_id_type=MESH,
        )

    def whole(x, h, group):
        count = PER - 1 if OWN // PER == group else PER
        s = pl.ds(group * PER * msg, count * msg)
        return pltpu.make_async_remote_copy(
            src_ref=send.at[x, h, s],
            dst_ref=recv.at[x, h, s],
            send_sem=send_sem.at[x, h, group],
            recv_sem=recv_sem.at[x, h, group],
            device_id={"dom": dom_at(0, 1)},
            device_id_type=MESH,
        )

    def post(x, h, group, values):
        for t in range(cols // 128):
            blocks = [values[g * msg : (g + 1) * msg, t * 128 : (t + 1) * 128] for g in range(per_tile)]
            for p, out in enumerate(swap_blocks(blocks, slots)):
                j = group * PER + t * per_tile + p
                if j != OWN:
                    send[x, h, j * msg : (j + 1) * msg, :] = out
        for j in range(group * PER, (group + 1) * PER):
            if j != OWN:
                message(x, h, j).start()

    def fetch(x, h, group):
        whole(x, h, group).wait_recv()
        columns = []
        for t in range(cols // 128):
            first = group * PER + t * per_tile
            blocks = [recv[x, h, (first + p) * msg : (first + p + 1) * msg, :] for p in range(per_tile)]
            columns.append(jnp.concatenate(swap_blocks(blocks, slots), axis=0))
        return jnp.concatenate(columns, axis=1)

    def gather(it, h):
        for group in range(2):
            s = slice(group * cols, (group + 1) * cols)
            post(2 * it, h, group, exact(yb[rows_of(h), :], yb[lows_of(h), :], onehot[:, s], NN))

    def scatter(it, h):
        total = None
        for group in range(2):
            s = slice(group * cols, (group + 1) * cols)
            hi, lo = parts(fetch(2 * it + 1, h, group))
            term = exact(hi, lo, onehot[:, s], NT)
            total = term if total is None else total + term
        y = y_t[rows_of(h), :] - STEP * total
        y_t[rows_of(h), :] = y
        hi, lo = parts(y)
        yb[rows_of(h), :] = hi
        yb[lows_of(h), :] = lo

    def primal(it, h):
        r = rows_of(h)
        for group in range(2):
            s = slice(group * cols, (group + 1) * cols)
            hi, lo = parts(fetch(2 * it, h, group) * live[0:1, s])
            g_t[r, :] += product(hi, lo, bnd_hi[s, :], bnd_lo[s, :], NN)
        f = f_t[r, :]
        new = jnp.clip(f - STEP * (cost_v[...] - g_t[r, :]), 0.0, cap_v[...])
        f_t[r, :] = new
        hi, lo = parts(2.0 * new - f)
        fb[r, :] = hi
        fb[lows_of(h), :] = lo
        for group in range(2):
            s = slice(group * cols, (group + 1) * cols)
            terms = product(fb[r, :], fb[lows_of(h), :], bnd_hi[s, :], bnd_lo[s, :], NT)
            post(2 * it + 1, h, group, terms * live[0:1, s])

    def halo(it, kind):
        return pltpu.make_async_remote_copy(
            src_ref=halo_send.at[it, kind],
            dst_ref=halo_recv.at[it, kind],
            send_sem=halo_send_sem.at[it, kind],
            recv_sem=halo_recv_sem.at[it, kind],
            device_id={"hour": nxt if kind else prv},
            device_id_type=MESH,
        )

    def prepare():
        cp_pres.wait()
        rows = 64
        bsize = pipes // presence.shape[1]

        def one_loc(i, _):
            @pl.when(lax.rem(i, step_loc // rows) == 0)
            def _():
                loc_copy(i // (step_loc // rows)).wait()

            s = pl.ds(pl.multiple_of(i * rows, rows), rows)
            for j in range(presence.shape[1]):
                c = slice(j * bsize, (j + 1) * bsize)
                scale = pres_s[i // (bsize // rows), j].astype(F32)
                hi, lo = parts(loc32[s, c] * scale)
                loc_hi[s, c] = hi
                loc_lo[s, c] = lo
            return 0

        lax.fori_loop(0, nodes // rows, one_loc, 0)
        g_t[...] = product(yb[:width, :], yb[width:, :], loc_hi[...], loc_lo[...], NN)

    def prepare_rest():
        cp_f.wait()
        for j in range(pipes // 128):
            s = slice(j * 128, (j + 1) * 128)
            f_t[:, s] = nat_f[s, :].T
        for i in range(n_bnd):
            bnd_copy(i).wait()
        for j, (dz, flip) in enumerate(BLOCKS):
            hi, lo = parts(bnd32[pl.ds(pl.multiple_of(dom_at(dz, flip) * slots, slots), slots), :])
            bnd_hi[j * slots : (j + 1) * slots, :] = hi
            bnd_lo[j * slots : (j + 1) * slots, :] = lo
        cp_d.wait()
        for j in range(nodes // 128):
            s = slice(j * 128, (j + 1) * 128)
            d_t[:, s] = nat_d[s, :].T
        cp_s.wait()
        s_t[...] = nat_s[...].T
        cp_cost.wait()
        cp_cap.wait()
        cp_scost.wait()
        cp_scap.wait()

    pl.semaphore_wait(barrier, PER * 2 - 1 + 2)

    row_of = lax.broadcasted_iota(jnp.int32, (width, store), 0)
    stor_cols = slice(all_slots, all_slots + store)

    def iteration(it, _):
        gather(it, 0)

        @pl.when(it > 0)
        def _():
            scatter(it - 1, 1)

        gather(it, 1)
        sd[...] = exact(yb[:width, :], yb[width:, :], onehot[:, stor_cols], NN)
        halo_send[it, 0] = sd[0:8, :]
        halo(it, 0).start()

        @pl.when(it == 0)
        def _():
            prepare()
            prepare_rest()

        @pl.when(it > 0)
        def _():
            g_t[...] = product(yb[:width, :], yb[width:, :], loc_hi[...], loc_lo[...], NN)

        halo(it, 0).wait_recv()
        now = sd[...]
        after = jnp.where(row_of == width - 1, halo_recv[it, 0, 0:1, :], pltpu.roll(now, width - 1, 0))
        s = s_t[...]
        new = jnp.clip(s - STEP * (scost_v[...] - (after - now)), 0.0, scap_v[...])
        s_t[...] = new
        bar = 2.0 * new - s
        w_t[...] = bar
        halo_send[it, 1] = bar[width - 8 :, :]
        halo(it, 1).start()

        primal(it, 0)
        primal(it, 1)

        halo(it, 1).wait_recv()
        bar = w_t[...]
        before = jnp.where(row_of == 0, halo_recv[it, 1, 7:8, :], pltpu.roll(bar, 1, 0))
        hi, lo = parts(before - bar)
        r = exact(hi, lo, onehot[:, stor_cols], NT)
        r = r + product(fb[:width, :], fb[width:, :], loc_hi[...], loc_lo[...], NT)
        y_t[...] = y_t[...] + STEP * (d_t[...] - r)
        scatter(it, 0)
        return 0

    lax.fori_loop(0, ITERS, iteration, 0)
    for j in range(pipes // 128):
        s = slice(j * 128, (j + 1) * 128)
        nat_f[s, :] = f_t[:, s].T
    nat_s[...] = s_t[...].T
    out_f = pltpu.make_async_copy(nat_f, flow_out, out_sem.at[0])
    out_f.start()
    out_s = pltpu.make_async_copy(nat_s, level_out, out_sem.at[1])
    out_s.start()
    scatter(ITERS - 1, 1)
    for j in range(nodes // 128):
        s = slice(j * 128, (j + 1) * 128)
        nat_y[s, :] = y_t[:, s].T
    out_y = pltpu.make_async_copy(nat_y, dual_out, out_sem.at[2])
    out_y.start()
    for x in range(2 * ITERS):
        for h in range(HALVES):
            for group in range(2):
                whole(x, h, group).wait_send()
    for it in range(ITERS):
        for kind in range(2):
            halo(it, kind).wait_send()
    out_f.wait()
    out_s.wait()
    out_y.wait()


def body(
    inc_local, inc_bound, bound_rows, bound_count, block_presence_mask, stor_nodes,
    flow0, stor0, dual0, demand, pipe_cost, pipe_cap, stor_cost, stor_cap,
):
    nodes, pipes = inc_local.shape
    store, width = stor0.shape
    peers, slots = bound_rows.shape[1:]
    all_slots = peers * slots
    half = width // HALVES
    n_msg = 2 * ITERS
    any_spec = pl.BlockSpec(memory_space=pl.ANY)
    vmem = pltpu.VMEM
    sem = pltpu.SemaphoreType.DMA
    args = (
        inc_local, inc_bound, bound_rows[0], bound_count, block_presence_mask, stor_nodes,
        flow0, stor0, dual0, demand, pipe_cost[None], pipe_cap[None], stor_cost[None], stor_cap[None],
    )
    return pl.pallas_call(
        kernel,
        out_shape=(
            jax.ShapeDtypeStruct((pipes, width), F32),
            jax.ShapeDtypeStruct((store, width), F32),
            jax.ShapeDtypeStruct((nodes, width), F32),
        ),
        in_specs=[any_spec] * len(args),
        out_specs=(any_spec,) * 3,
        scratch_shapes=[
            vmem((nodes, pipes), F32),
            vmem((all_slots, pipes), F32),
            vmem((nodes, pipes), BF16),
            vmem((nodes, pipes), BF16),
            vmem((all_slots, pipes), BF16),
            vmem((all_slots, pipes), BF16),
            vmem((pipes, width), F32),
            vmem((nodes, width), F32),
            vmem((nodes, width), F32),
            vmem((store, width), F32),
            vmem((peers, slots), jnp.int32),
            vmem((1, store), jnp.int32),
            vmem((1, pipes), F32),
            vmem((1, pipes), F32),
            vmem((1, store), F32),
            vmem((1, store), F32),
            pltpu.SMEM(bound_count.shape, jnp.int32),
            pltpu.SMEM(block_presence_mask.shape, jnp.int32),
            vmem((width, pipes), F32),
            vmem((width, nodes), F32),
            vmem((width, nodes), F32),
            vmem((width, store), F32),
            vmem((width, pipes), F32),
            vmem((2 * width, pipes), BF16),
            vmem((2 * width, nodes), BF16),
            vmem((width, store), F32),
            vmem((nodes, all_slots + store), BF16),
            vmem((8, all_slots), F32),
            vmem((width, store), F32),
            vmem((n_msg, HALVES, half * all_slots // 128, 128), F32),
            vmem((n_msg, HALVES, half * all_slots // 128, 128), F32),
            vmem((ITERS, 2, 8, store), F32),
            vmem((ITERS, 2, 8, store), F32),
            sem((12,)),
            sem((8,)),
            sem((4,)),
            sem((3,)),
            sem((n_msg, HALVES, 2)),
            sem((n_msg, HALVES, 2)),
            sem((ITERS, 2)),
            sem((ITERS, 2)),
        ],
        compiler_params=pltpu.CompilerParams(
            collective_id=0, has_side_effects=True, vmem_limit_bytes=56 * 2**20
        ),
    )(*args)


def solution(mesh):
    placed = (
        P("dom", None),
        P("dom", None),
        P("dom", None, None),
        P(),
        P("dom", None),
        P("dom", None),
        P("dom", "hour"),
        P("dom", "hour"),
        P("dom", "hour"),
        P("dom", "hour"),
        P("dom"),
        P("dom"),
        P("dom"),
        P("dom"),
    )
    return jax.shard_map(
        body,
        mesh=mesh,
        in_specs=placed,
        out_specs=(P("dom", "hour"), P("dom", "hour"), P("dom", "hour")),
        check_vma=False,
    )
```

profile of v0, /device:TPU:1, one launch (start us, length us, event | category | flops | bytes accessed | tf_op | source)
XLA Modules:
  0.0 53.1 jit_solution(1187525386613501758)
XLA Ops:
  0.6 46.8 %shard_map.157 = (f32[2048,128]{1,0:T(8,128)}, f32[128,128]{1,0:T(8,128)}, f32[1024,128]{1,0:T(8,128)}) custom-call(f32[1024,2048]{1,0:T(8,128)} %inc_local.1, f32[512,2048]{1,0:T(8,128)} %inc_bound.1, s32[16,32]{1,0:T(8,128)} %bitcast.5, s32[16,16]{1,0:T(8,128)} %bound_count.1, s32[4,8]{1,0:T(4,128)} %presence.1, s32[1,128]{1,0:T(1,128)} %stor_nodes.1, ...), custom_call_target="tpu_custom_call" | custom-call | tf_op jit(solution)/shard_map/pallas_call | solution.py:392
  47.5 2.3 %copy.20 = f32[2048,128]{1,0:T(8,128)} copy(f32[2048,128]{1,0:T(8,128)} %get-tuple-element.6) | data formatting | bytes 2097152
  49.7 1.5 %copy.21 = f32[128,128]{1,0:T(8,128)} copy(f32[128,128]{1,0:T(8,128)} %get-tuple-element.7) | data formatting | bytes 131072
  51.2 1.9 %copy.22 = f32[1024,128]{1,0:T(8,128)} copy(f32[1024,128]{1,0:T(8,128)} %get-tuple-element.8) | data formatting | bytes 1048576
where the time goes:
time: 53.3 us; the launch traced here: 53.1 us
  Pallas kernels  46.8 us (88%)
  local copies, waits for them, and re-layouts  5.6 us (11%)
  between operations  0.65 us (1%)
    pallas_call x1, Pallas kernels, body(): pl.pallas_call(kernel, out_shape=(jax.ShapeDtypeStruct((pipes, width), F3...  46.8 us
    unnamed x3, local copies, waits for them, and re-layouts  5.6 us

commit v1 on v0

--- a/solution.py
+++ b/solution.py
@@ -63,7 +63,7 @@
     inc_local, inc_bound, bound_rows, bound_count, presence, stor_nodes,
     flow0, stor0, dual0, demand, pipe_cost, pipe_cap, stor_cost, stor_cap,
     flow_out, level_out, dual_out,
-    loc32, bnd32, loc_hi, loc_lo, bnd_hi, bnd_lo,
+    loc32, bnd32, loc_hi, loc_lo, bnd_hi, bnd_lo, bt_hi, bt_lo,
     nat_f, nat_y, nat_d, nat_s, rows_v, stor_v, cost_v, cap_v, scost_v, scap_v, count_s, pres_s,
     f_t, y_t, d_t, s_t, g_t, fb, yb, sd, onehot, live, w_t,
     send, recv, halo_send, halo_recv,
@@ -207,17 +207,13 @@
         return jnp.concatenate(columns, axis=1)
 
     def gather(it, h):
+        values = exact(yb[rows_of(h), :], yb[lows_of(h), :], onehot[:, :all_slots], NN)
         for group in range(2):
-            s = slice(group * cols, (group + 1) * cols)
-            post(2 * it, h, group, exact(yb[rows_of(h), :], yb[lows_of(h), :], onehot[:, s], NN))
+            post(2 * it, h, group, values[:, group * cols : (group + 1) * cols])
 
     def scatter(it, h):
-        total = None
-        for group in range(2):
-            s = slice(group * cols, (group + 1) * cols)
-            hi, lo = parts(fetch(2 * it + 1, h, group))
-            term = exact(hi, lo, onehot[:, s], NT)
-            total = term if total is None else total + term
+        hi, lo = parts(jnp.concatenate([fetch(2 * it + 1, h, group) for group in range(2)], axis=1))
+        total = exact(hi, lo, onehot[:, :all_slots], NT)
         y = y_t[rows_of(h), :] - STEP * total
         y_t[rows_of(h), :] = y
         hi, lo = parts(y)
@@ -236,10 +232,10 @@
         hi, lo = parts(2.0 * new - f)
         fb[r, :] = hi
         fb[lows_of(h), :] = lo
+        terms = product(fb[r, :], fb[lows_of(h), :], bt_hi[...], bt_lo[...], NN) * live[0:1, :]
         for group in range(2):
             s = slice(group * cols, (group + 1) * cols)
-            terms = product(fb[r, :], fb[lows_of(h), :], bnd_hi[s, :], bnd_lo[s, :], NT)
-            post(2 * it + 1, h, group, terms * live[0:1, s])
+            post(2 * it + 1, h, group, terms[:, s])
 
     def halo(it, kind):
         return pltpu.make_async_remote_copy(
@@ -284,6 +280,8 @@
             hi, lo = parts(bnd32[pl.ds(pl.multiple_of(dom_at(dz, flip) * slots, slots), slots), :])
             bnd_hi[j * slots : (j + 1) * slots, :] = hi
             bnd_lo[j * slots : (j + 1) * slots, :] = lo
+        bt_hi[...] = bnd_hi[...].T
+        bt_lo[...] = bnd_lo[...].T
         cp_d.wait()
         for j in range(nodes // 128):
             s = slice(j * 128, (j + 1) * 128)
@@ -372,6 +370,19 @@
     out_y.wait()
 
 
+def store_all(flow_in, level_in, dual_in, flow_out, level_out, dual_out, flow, level, dual, sems, in_sems):
+    pairs = ((flow, flow_out), (level, level_out), (dual, dual_out))
+    copies = [pltpu.make_async_copy(a, b, sems.at[i]) for i, (a, b) in enumerate(pairs)]
+    loads = [pltpu.make_async_copy(a, b, in_sems.at[i]) for i, (a, b) in enumerate(((flow_in, flow), (level_in, level), (dual_in, dual)))]
+    for c in loads:
+        c.start()
+    for a, c in zip(loads, copies):
+        a.wait()
+        c.start()
+    for c in copies:
+        c.wait()
+
+
 def body(
     inc_local, inc_bound, bound_rows, bound_count, block_presence_mask, stor_nodes,
     flow0, stor0, dual0, demand, pipe_cost, pipe_cap, stor_cost, stor_cap,
@@ -389,7 +400,7 @@
         inc_local, inc_bound, bound_rows[0], bound_count, block_presence_mask, stor_nodes,
         flow0, stor0, dual0, demand, pipe_cost[None], pipe_cap[None], stor_cost[None], stor_cap[None],
     )
-    return pl.pallas_call(
+    results = pl.pallas_call(
         kernel,
         out_shape=(
             jax.ShapeDtypeStruct((pipes, width), F32),
@@ -405,6 +416,8 @@
             vmem((nodes, pipes), BF16),
             vmem((all_slots, pipes), BF16),
             vmem((all_slots, pipes), BF16),
+            vmem((pipes, all_slots), BF16),
+            vmem((pipes, all_slots), BF16),
             vmem((pipes, width), F32),
             vmem((nodes, width), F32),
             vmem((nodes, width), F32),
@@ -445,6 +458,13 @@
             collective_id=0, has_side_effects=True, vmem_limit_bytes=56 * 2**20
         ),
     )(*args)
+    return pl.pallas_call(
+        store_all,
+        out_shape=tuple(jax.ShapeDtypeStruct(r.shape, r.dtype) for r in results),
+        in_specs=[any_spec] * 3,
+        out_specs=(any_spec,) * 3,
+        scratch_shapes=[vmem(r.shape, F32) for r in results] + [sem((3,)), sem((3,))],
+    )(*results)
 
 
 def solution(mesh):

time: 53.3 us -> 46.3 us (0.87)
  local copies, waits for them, and re-layouts: 5.6 us -> 0 us
  Pallas kernels: 46.8 us -> 45.6 us
    unnamed x3 -> x0, local copies, waits for them, and re-layouts: 5.6 us -> none
    pallas_call x1, Pallas kernels: 46.8 us -> 43.2 us  [body(): pl.pallas_call(kernel, out_shape=(jax.ShapeDtypeStruct((pipes, width), F3...]
    pallas_call x0 -> x1, Pallas kernels: none -> 2.44 us  [body(): pl.pallas_call(store_all, out_shape=tuple((jax.ShapeDtypeStruct(r.shape,...]
where the time goes in v1:
time: 46.3 us; the launch traced here: 46.2 us
  Pallas kernels  45.6 us (98%)
  between operations  0.64 us (1%)
    pallas_call x1, Pallas kernels, body(): pl.pallas_call(kernel, out_shape=(jax.ShapeDtypeStruct((pipes, width), F3...  43.2 us
    pallas_call x1, Pallas kernels, body(): pl.pallas_call(store_all, out_shape=tuple((jax.ShapeDtypeStruct(r.shape,...  2.44 us

profile of v1, /device:TPU:1, one launch (start us, length us, event | category | flops | bytes accessed | tf_op | source)
XLA Modules:
  0.0 46.2 jit_solution(12145877166243555098)
XLA Ops:
  0.6 43.2 %shard_map.157 = (f32[2048,128]{1,0:T(8,128)}, f32[128,128]{1,0:T(8,128)}, f32[1024,128]{1,0:T(8,128)}) custom-call(f32[1024,2048]{1,0:T(8,128)} %inc_local.1, f32[512,2048]{1,0:T(8,128)} %inc_bound.1, s32[16,32]{1,0:T(8,128)} %bitcast.5, s32[16,16]{1,0:T(8,128)} %bound_count.1, s32[4,8]{1,0:T(4,128)} %presence.1, s32[1,128]{1,0:T(1,128)} %stor_nodes.1, ...), custom_call_target="tpu_custom_call" | custom-call | tf_op jit(solution)/shard_map/pallas_call | solution.py:403
  43.8 2.4 %shard_map.158 = (f32[2048,128]{1,0:T(8,128)}, f32[128,128]{1,0:T(8,128)}, f32[1024,128]{1,0:T(8,128)}) custom-call(f32[2048,128]{1,0:T(8,128)} %get-tuple-element.6.flow_in, f32[128,128]{1,0:T(8,128)} %get-tuple-element.7.level_in, f32[1024,128]{1,0:T(8,128)} %get-tuple-element.8.dual_in), custom_call_target="tpu_custom_call" | custom-call | tf_op jit(solution)/shard_map/pallas_call | solution.py:461

commit v2 on v1

--- a/solution.py
+++ b/solution.py
@@ -15,8 +15,8 @@
 NT = (((1,), (1,)), ((), ()))
 
 GROUPS = (
-    ((4, 0), (4, 1), (3, 0), (3, 1), (-3, 0), (-3, 1), (0, 1), (0, 0)),
-    ((2, 0), (2, 1), (-2, 0), (-2, 1), (1, 0), (1, 1), (-1, 0), (-1, 1)),
+    ((4, 1), (4, 0), (3, 1), (3, 0), (-3, 1), (-3, 0), (0, 1), (0, 0)),
+    ((2, 1), (2, 0), (-2, 1), (-2, 0), (1, 1), (1, 0), (-1, 1), (-1, 0)),
 )
 BLOCKS = GROUPS[0] + GROUPS[1]
 PER = len(GROUPS[0])

time: 46.3 us -> 45.8 us (0.989)
  Pallas kernels: 45.6 us -> 45 us
    pallas_call x1, Pallas kernels: 43.2 us -> 42.6 us  [body(): pl.pallas_call(kernel, out_shape=(jax.ShapeDtypeStruct((pipes, width), F3...]
where the time goes in v2:
time: 45.8 us; the launch traced here: 45.7 us
  Pallas kernels  45 us (98%)
  between operations  0.64 us (1%)
    pallas_call x1, Pallas kernels, body(): pl.pallas_call(kernel, out_shape=(jax.ShapeDtypeStruct((pipes, width), F3...  42.6 us
    pallas_call x1, Pallas kernels, body(): pl.pallas_call(store_all, out_shape=tuple((jax.ShapeDtypeStruct(r.shape,...  2.44 us

profile of v2, /device:TPU:1, one launch (start us, length us, event | category | flops | bytes accessed | tf_op | source)
XLA Modules:
  0.0 45.7 jit_solution(4447599164220569661)
XLA Ops:
  0.6 42.6 %shard_map.157 = (f32[2048,128]{1,0:T(8,128)}, f32[128,128]{1,0:T(8,128)}, f32[1024,128]{1,0:T(8,128)}) custom-call(f32[1024,2048]{1,0:T(8,128)} %inc_local.1, f32[512,2048]{1,0:T(8,128)} %inc_bound.1, s32[16,32]{1,0:T(8,128)} %bitcast.5, s32[16,16]{1,0:T(8,128)} %bound_count.1, s32[4,8]{1,0:T(4,128)} %presence.1, s32[1,128]{1,0:T(1,128)} %stor_nodes.1, ...), custom_call_target="tpu_custom_call" | custom-call | tf_op jit(solution)/shard_map/pallas_call | solution.py:403
  43.3 2.4 %shard_map.158 = (f32[2048,128]{1,0:T(8,128)}, f32[128,128]{1,0:T(8,128)}, f32[1024,128]{1,0:T(8,128)}) custom-call(f32[2048,128]{1,0:T(8,128)} %get-tuple-element.6.flow_in, f32[128,128]{1,0:T(8,128)} %get-tuple-element.7.level_in, f32[1024,128]{1,0:T(8,128)} %get-tuple-element.8.dual_in), custom_call_target="tpu_custom_call" | custom-call | tf_op jit(solution)/shard_map/pallas_call | solution.py:461

commit v3 on v2

--- a/solution.py
+++ b/solution.py
@@ -353,11 +353,14 @@
     out_s = pltpu.make_async_copy(nat_s, level_out, out_sem.at[1])
     out_s.start()
     scatter(ITERS - 1, 1)
+    out_y = []
     for j in range(nodes // 128):
         s = slice(j * 128, (j + 1) * 128)
         nat_y[s, :] = y_t[:, s].T
-    out_y = pltpu.make_async_copy(nat_y, dual_out, out_sem.at[2])
-    out_y.start()
+        if j % 4 == 3:
+            part = slice((j - 3) * 128, (j + 1) * 128)
+            out_y.append(pltpu.make_async_copy(nat_y.at[part], dual_out.at[part], out_sem.at[2 + j // 4]))
+            out_y[-1].start()
     for x in range(2 * ITERS):
         for h in range(HALVES):
             for group in range(2):
@@ -367,19 +370,24 @@
             halo(it, kind).wait_send()
     out_f.wait()
     out_s.wait()
-    out_y.wait()
+    for c in out_y:
+        c.wait()
 
 
 def store_all(flow_in, level_in, dual_in, flow_out, level_out, dual_out, flow, level, dual, sems, in_sems):
-    pairs = ((flow, flow_out), (level, level_out), (dual, dual_out))
-    copies = [pltpu.make_async_copy(a, b, sems.at[i]) for i, (a, b) in enumerate(pairs)]
-    loads = [pltpu.make_async_copy(a, b, in_sems.at[i]) for i, (a, b) in enumerate(((flow_in, flow), (level_in, level), (dual_in, dual)))]
+    pieces = []
+    for source, held, target in ((flow_in, flow, flow_out), (dual_in, dual, dual_out), (level_in, level, level_out)):
+        rows = min(512, source.shape[0])
+        for k in range(source.shape[0] // rows):
+            pieces.append((source, held, target, pl.ds(k * rows, rows)))
+    loads = [pltpu.make_async_copy(a.at[s], b.at[s], in_sems.at[i]) for i, (a, b, _, s) in enumerate(pieces)]
+    stores = [pltpu.make_async_copy(b.at[s], c.at[s], sems.at[i]) for i, (_, b, c, s) in enumerate(pieces)]
     for c in loads:
         c.start()
-    for a, c in zip(loads, copies):
+    for a, c in zip(loads, stores):
         a.wait()
         c.start()
-    for c in copies:
+    for c in stores:
         c.wait()
 
 
@@ -448,7 +456,7 @@
             sem((12,)),
             sem((8,)),
             sem((4,)),
-            sem((3,)),
+            sem((2 + nodes // 512,)),
             sem((n_msg, HALVES, 2)),
             sem((n_msg, HALVES, 2)),
             sem((ITERS, 2)),
@@ -463,7 +471,7 @@
         out_shape=tuple(jax.ShapeDtypeStruct(r.shape, r.dtype) for r in results),
         in_specs=[any_spec] * 3,
         out_specs=(any_spec,) * 3,
-        scratch_shapes=[vmem(r.shape, F32) for r in results] + [sem((3,)), sem((3,))],
+        scratch_shapes=[vmem(r.shape, F32) for r in results] + [sem((8,)), sem((8,))],
     )(*results)
 
 

time: 45.8 us -> 45.5 us (level)
  no operation moved by 1% of the time
where the time goes in v3:
time: 45.5 us; the launch traced here: 45.4 us
  Pallas kernels  44.8 us (98%)
  between operations  0.64 us (1%)
    pallas_call x1, Pallas kernels, body(): pl.pallas_call(kernel, out_shape=(jax.ShapeDtypeStruct((pipes, width), F3...  42.5 us
    pallas_call x1, Pallas kernels, body(): pl.pallas_call(store_all, out_shape=tuple((jax.ShapeDtypeStruct(r.shape,...  2.24 us

profile of v3, /device:TPU:1, one launch (start us, length us, event | category | flops | bytes accessed | tf_op | source)
XLA Modules:
  0.0 45.4 jit_solution(12561975028725785253)
XLA Ops:
  0.6 42.5 %shard_map.157 = (f32[2048,128]{1,0:T(8,128)}, f32[128,128]{1,0:T(8,128)}, f32[1024,128]{1,0:T(8,128)}) custom-call(f32[1024,2048]{1,0:T(8,128)} %inc_local.1, f32[512,2048]{1,0:T(8,128)} %inc_bound.1, s32[16,32]{1,0:T(8,128)} %bitcast.5, s32[16,16]{1,0:T(8,128)} %bound_count.1, s32[4,8]{1,0:T(4,128)} %presence.1, s32[1,128]{1,0:T(1,128)} %stor_nodes.1, ...), custom_call_target="tpu_custom_call" | custom-call | tf_op jit(solution)/shard_map/pallas_call | solution.py:411
  43.2 2.2 %shard_map.158 = (f32[2048,128]{1,0:T(8,128)}, f32[128,128]{1,0:T(8,128)}, f32[1024,128]{1,0:T(8,128)}) custom-call(f32[2048,128]{1,0:T(8,128)} %get-tuple-element.6.flow_in, f32[128,128]{1,0:T(8,128)} %get-tuple-element.7.level_in, f32[1024,128]{1,0:T(8,128)} %get-tuple-element.8.dual_in), custom_call_target="tpu_custom_call" | custom-call | tf_op jit(solution)/shard_map/pallas_call | solution.py:469
